TPU v7x, 32 devices: a whole 2x2x4 slice. The times are simulated.
32 devices in a mesh: seq: 16 (over z, y, core), head: 2 (over x).
Axes of the slice: x: 2, y: 2, z: 4, core: 2. Of those that a mesh axis runs over, the one named last changes fastest.
Arguments:
- tokens: bfloat16 [2048, 2880], P('seq'), may hold values from -80 to 80
- gain: float32 [2880], replicated, may hold values from 0.1 to 1.9
- w_query: bfloat16 [2880, 1024], P('seq', 'head'), may hold values from -4 to 4
- w_key: bfloat16 [2880, 128], P('seq', 'head'), may hold values from -1 to 1
- w_value: bfloat16 [2880, 128], P('seq', 'head'), may hold values from -0.109375 to 0.109375
- w_out: bfloat16 [2880, 1024], P('seq', 'head'), may hold values from -0.1875 to 0.1875
- w_gate: float32 [2880], replicated, may hold values from -0.109375 to 0.109375
- steering: bfloat16 [16, 2880], replicated, may hold values from -5 to 5
- segment_ids: int32 [2048], P('seq'), may hold values from 0 to 7, never falling along the last dimension, each value on 1 to 512 neighbouring positions
- steer_index: int32 [2048], P('seq'), may hold values from 0 to 15
- grad_out: bfloat16 [2048, 2880], P('seq'), may hold values from -6 to 6
Outputs:
- layer_out: bfloat16 [2048, 2880], P('seq', 'head')
- grad_tokens: bfloat16 [2048, 2880], P('seq', 'head')
- steer_grad: float32 [16, 2880], P(None, 'head')
Inputs may be any that keep to these rules, and one draw needn't show every extreme that they name: `segment_ids`: the ids never fall along the tokens; each id names one packed document of at most 512 tokens.
All inputs are finite; a program needn't handle non-finite values.
Results may differ from a plain program's by a relative error of at most 0.011.
Values may be sent and summed in bfloat16 or wider, within the bound.
A program may use at most 64 MiB of HBM per device.

v0:
```python
import functools
import jax
import jax.numpy as jnp
from jax import lax
from jax.experimental import pallas as pl
from jax.experimental.pallas import tpu as pltpu
from jax.sharding import PartitionSpec as P

WIN = 128
EPSILON = 1e-05
HIGHEST = lax.Precision.HIGHEST
MESH = pl.DeviceIdType.MESH
PIECES = 3
ROWS_OF_CHIPS = 4
F32 = jnp.float32
BF16 = jnp.bfloat16


def dot(left, right):
    return jnp.dot(left, right, preferred_element_type=F32)


def dot_t(left, right):
    return lax.dot_general(left, right, (((1,), (1,)), ((), ())), preferred_element_type=F32)


def t_dot(left, right):
    return lax.dot_general(left, right, (((0,), (0,)), ((), ())), preferred_element_type=F32)


def kernel(
    S,
    H,
    tok_ref,
    vec_ref,
    wq_ref,
    wk_ref,
    wv_ref,
    wo_ref,
    steer_ref,
    seg_ref,
    sidx_ref,
    go_ref,
    lay_ref,
    gtok_ref,
    sgrad_ref,
    qbuf,
    obuf,
    tok_p,
    go_p,
    go_c,
    norm_c,
    vec_p,
    steer_p,
    qacc,
    gmacc,
    kvall,
    segbuf,
    pbuf,
    abuf,
    arecv,
    gbuf,
    grecv,
    rbuf,
    rrecv,
    hgsend,
    hgrecv,
    sacc,
    srecv,
    qsend,
    qrecv,
    osend,
    orecv,
    segsem,
    kvsem,
    hgsem,
    asend,
    arsem,
    gsend,
    grsem,
    rsend,
    rrsem,
    ssend,
    srsem,
):
    T, D = tok_ref.shape
    rows, group_cols = wq_ref.shape
    hd = wk_ref.shape[1]
    heads = group_cols // hd
    scale = hd ** (-0.5)
    share = S // H // 2
    C = S // 2
    half = C // 2
    Y = C // ROWS_OF_CHIPS
    steps = sacc.shape[0] - 1
    steer_count = steer_ref.shape[0]

    me = lax.axis_index("seq")
    h = lax.axis_index("head")
    core = me % 2
    chip = me // 2
    z, y = chip // Y, chip % Y
    odd = z % 2
    inner = z * (Y - 1) + (1 - odd) * (y - 1) + odd * (Y - 1 - y)
    outer = ROWS_OF_CHIPS * (Y - 1) + (ROWS_OF_CHIPS - 1 - z)
    pos = jnp.where(y == 0, outer, inner)

    def at(place):
        p = place % C
        zi = p // (Y - 1)
        o = p % (Y - 1)
        yi = jnp.where(zi % 2 == 0, 1 + o, Y - 1 - o)
        last = p >= ROWS_OF_CHIPS * (Y - 1)
        zz = jnp.where(last, ROWS_OF_CHIPS - 1 - (p - ROWS_OF_CHIPS * (Y - 1)), zi)
        yy = jnp.where(last, 0, yi)
        return (zz * Y + yy) * 2 + core

    cw, ccw = at(pos + 1), at(pos + C - 1)
    other = 1 - 2 * core
    sib = me + other
    after, before = (me + 1) % S, (me + S - 1) % S
    pairs = []
    for k in range(steps):
        bit = (me // (1 << k)) % 2
        pairs.append(me + (1 - 2 * bit) * (1 << k))
    peers = [(h + d) % H for d in range(1, H)]

    barrier = pltpu.get_barrier_semaphore()
    for target in [cw, ccw, sib, after, before] + pairs:
        pl.semaphore_signal(barrier, inc=1, device_id=(target, h), device_id_type=MESH)
    for peer in peers:
        pl.semaphore_signal(barrier, inc=1, device_id=(me, peer), device_id_type=MESH)

    qbuf[me] = jnp.zeros(qbuf.shape[1:], BF16)
    obuf[me] = jnp.zeros(obuf.shape[1:], BF16)
    qbuf[me, :rows, :group_cols] = wq_ref[...]
    qbuf[me, :rows, group_cols:] = jnp.concatenate([wk_ref[...], wv_ref[...]], axis=1)
    obuf[me, :rows, :] = wo_ref[...]
    segbuf[1] = jnp.broadcast_to(seg_ref[...], segbuf.shape[1:])

    pl.semaphore_wait(barrier, 5 + steps + H - 1)

    def remote(src, dst, send, recv, seq, head):
        return pltpu.make_async_remote_copy(
            src_ref=src,
            dst_ref=dst,
            send_sem=send,
            recv_sem=recv,
            device_id=(seq, head),
            device_id_type=MESH,
        )

    targets = (cw, ccw, sib)
    piece = qbuf.shape[1] // PIECES

    def q_copy(slot, way, i):
        part = pl.ds(i * piece, piece)
        return remote(
            qbuf.at[slot, part],
            qbuf.at[slot, part],
            qsend.at[way, slot, i],
            qrecv.at[slot, i],
            targets[way],
            h,
        )

    def o_copy(slot, way, i):
        part = pl.ds(i * piece, piece)
        return remote(
            obuf.at[slot, part],
            obuf.at[slot, part],
            osend.at[way, slot, i],
            orecv.at[slot, i],
            targets[way],
            h,
        )

    every = range(PIECES)
    for i in every:
        for way in range(3):
            q_copy(me, way, i).start()
    seg_copy = remote(segbuf.at[1], segbuf.at[0], segsem.at[0], segsem.at[1], after, h)
    seg_copy.start()

    def q_fwd(t):
        a, b = at(pos + C - t), at(pos + t)
        for i in every:
            q_copy(a, 0, i).wait_recv()
            q_copy(a, 0, i).start()
            q_copy(a, 2, i).start()
            q_copy(b, 1, i).wait_recv()

            @pl.when(t < half - 1)
            def _():
                q_copy(b, 1, i).start()

            q_copy(b, 2, i).start()

    def o_fwd(t):
        b, a = at(pos + t), at(pos + C - t)
        for i in every:
            o_copy(b, 1, i).wait_recv()
            o_copy(b, 1, i).start()
            o_copy(b, 2, i).start()
            o_copy(a, 0, i).wait_recv()

            @pl.when(t < half - 1)
            def _():
                o_copy(a, 0, i).start()

            o_copy(a, 2, i).start()

    tokens = tok_ref[...].astype(F32)
    inverse = lax.rsqrt(jnp.sum(tokens * tokens, axis=1, keepdims=True) * (1.0 / D) + EPSILON)
    normed = (tokens * inverse * vec_ref[0:1, :]).astype(BF16)
    norm_c[...] = jnp.zeros(norm_c.shape, BF16)
    for c in range(S):
        norm_c[c, :, :rows] = normed[:, c * rows : (c + 1) * rows]

    def q_acc(slot):
        qacc[...] += dot(norm_c[slot], qbuf[slot])

    def q_sib(slot):
        for i in every:
            q_copy(slot, 2, i).wait_recv()
        q_acc(slot)

    def q_work(t):
        a, b = at(pos + C - t), at(pos + t)
        q_acc(a)
        q_acc(b)
        q_sib(a + other)
        q_sib(b + other)

    q_fwd(1)
    qacc[...] = dot(norm_c[me], qbuf[me])
    q_sib(sib)
    gate = jax.nn.sigmoid(
        jnp.sum(normed.astype(F32) * vec_ref[1:2, :], axis=1, keepdims=True)
    )
    for ref in (tok_p, go_p, go_c, vec_p, steer_p):
        ref[...] = jnp.zeros(ref.shape, ref.dtype)
    for c in range(S // 2):
        cols = slice(c * 2 * rows, (c + 1) * 2 * rows)
        tok_p[c, :, : 2 * rows] = tok_ref[:, cols]
        go_p[c, :, : 2 * rows] = go_ref[:, cols]
        vec_p[c, :, : 2 * rows] = vec_ref[:, cols]
        steer_p[c, :, : 2 * rows] = steer_ref[:, cols]
    for c in range(S):
        go_c[c, :, :rows] = go_ref[:, c * rows : (c + 1) * rows]

    def q_both(t, carry):
        q_fwd(t)
        q_work(t - 1)
        return carry

    lax.fori_loop(2, half, q_both, 0)
    for i in every:
        for way in range(3):
            o_copy(me, way, i).start()
    q_work(half - 1)
    far = at(pos + half)
    for i in every:
        q_copy(far, 0, i).wait_recv()
        q_copy(far, 2, i).start()
    q_acc(far)
    q_sib(far + other)

    qkv = qacc[...].astype(BF16)
    kvall[T:] = qkv[:, group_cols:]
    kv_copy = remote(
        kvall.at[pl.ds(T, T)], kvall.at[pl.ds(0, T)], kvsem.at[0], kvsem.at[1], after, h
    )
    kv_copy.start()

    same = lax.broadcasted_iota(jnp.int32, (T, T), 0) == lax.broadcasted_iota(jnp.int32, (T, T), 1)

    def column(row):
        return jnp.sum(jnp.where(same, jnp.broadcast_to(row, (T, T)), 0), axis=1, keepdims=True)

    sidx_row = sidx_ref[...]
    sidx_col = column(sidx_row)
    one_hot_b = (
        (lax.broadcasted_iota(jnp.int32, (T, steer_count), 1) == sidx_col).astype(F32).astype(BF16)
    )
    one_hot_t = (lax.broadcasted_iota(jnp.int32, (steer_count, T), 0) == sidx_row).astype(F32)

    def logit_step(c, total):
        return total + go_p[c].astype(F32) * dot(one_hot_b, steer_p[c])

    logit_sum = lax.fori_loop(0, S // 2, logit_step, jnp.zeros(go_p.shape[1:], F32))
    grad_logit = gate * (1.0 - gate) * jnp.sum(logit_sum, axis=1, keepdims=True)

    @pl.loop(0, share)
    def _(j):
        sacc[0, j] = jnp.dot(
            one_hot_t,
            gate * go_p[h * share + j].astype(F32),
            precision=HIGHEST,
            preferred_element_type=F32,
        )

    def s_copy(k):
        return remote(sacc.at[k], srecv.at[k], ssend.at[k], srsem.at[k], pairs[k], h)

    def s_finish(k):
        s_copy(k).wait_recv()
        sacc[k + 1] = sacc[k] + srecv[k]

    seg_copy.wait_recv()
    halo_seg = jnp.where(me > 0, segbuf[0, 0:1, :], -1)
    seg_row = seg_ref[...]
    query_seg = column(seg_row)
    key_seg = jnp.concatenate([halo_seg, seg_row], axis=1)
    distance = (
        lax.broadcasted_iota(jnp.int32, (T, 2 * T), 0)
        - lax.broadcasted_iota(jnp.int32, (T, 2 * T), 1)
        + T
    )
    mask = (distance >= 0) & (distance < WIN) & (query_seg == key_seg)

    kv_copy.wait_recv()
    keys = kvall[:, :hd]
    values = kvall[:, hd:]
    mixed_parts = []
    for i in range(heads):
        scores = dot_t(qkv[:, i * hd : (i + 1) * hd], keys) * scale
        scores = jnp.where(mask, scores, -1e30)
        raised = jnp.exp(scores - jnp.max(scores, axis=1, keepdims=True))
        probs = raised / jnp.sum(raised, axis=1, keepdims=True)
        pbuf[i] = probs
        mixed_parts.append(dot(probs.astype(BF16), values).astype(BF16))
        if i == heads // 2 - 1:
            o_fwd(1)
        if i == heads - 1:
            o_fwd(2)
    mixed = jnp.concatenate(mixed_parts, axis=1)

    def joined(low, high):
        fill = jnp.zeros((T, abuf.shape[2] - 2 * rows), F32)
        return jnp.concatenate([low[:, :rows], high[:, :rows], fill], axis=1).astype(BF16)

    def a_copy(pair):
        return remote(
            abuf.at[pair],
            arecv.at[h, pair % share],
            asend.at[pair],
            arsem.at[h, pair % share],
            me,
            pair // share,
        )

    def o_acc(slot):
        for i in every:
            o_copy(slot + other, 2, i).wait_recv()
        pair = slot // 2
        low, high = obuf[2 * pair], obuf[2 * pair + 1]
        abuf[pair] = joined(dot_t(mixed, low), dot_t(mixed, high))

        @pl.when(pair // share != h)
        def _():
            a_copy(pair).start()

        gmacc[...] += dot(go_c[2 * pair], low) + dot(go_c[2 * pair + 1], high)

    def o_work(t):
        o_acc(at(pos + t))
        o_acc(at(pos + C - t))

    gmacc[...] = jnp.zeros(gmacc.shape, F32)
    o_acc(me)
    o_work(1)

    def o_both(t, carry):
        o_fwd(t)
        o_work(t - 1)
        return carry

    lax.fori_loop(3, half, o_both, 0)
    for i in every:
        o_copy(far, 1, i).wait_recv()
        o_copy(far, 2, i).start()
    s_copy(0).start()
    o_work(half - 1)
    o_acc(far)

    grad_mixed = gmacc[...].astype(BF16)
    grad_query = []
    grad_keys = jnp.zeros((2 * T, hd), F32)
    grad_values = jnp.zeros((2 * T, hd), F32)
    for i in range(heads):
        part = grad_mixed[:, i * hd : (i + 1) * hd]
        probs = pbuf[i]
        grad_prob = dot_t(part, values)
        delta = jnp.sum(probs * grad_prob, axis=1, keepdims=True)
        grad_scores = (probs * (grad_prob - delta) * scale).astype(BF16)
        grad_query.append(dot(grad_scores, keys).astype(BF16))
        grad_keys = grad_keys + t_dot(grad_scores, qkv[:, i * hd : (i + 1) * hd])
        grad_values = grad_values + t_dot(probs.astype(BF16), part)
    grad_kv = jnp.concatenate([grad_keys, grad_values], axis=1)
    hgsend[...] = grad_kv[:T].astype(BF16)
    hg_copy = remote(hgsend, hgrecv, hgsem.at[0], hgsem.at[1], before, h)
    hg_copy.start()
    s_finish(0)
    s_copy(1).start()

    for j in range(share):
        c = h * share + j
        total = abuf[c].astype(F32)
        for peer in peers:
            remote(
                abuf.at[c], arecv.at[peer, j], asend.at[c], arsem.at[peer, j], me, peer
            ).wait_recv()
            total = total + arecv[peer, j].astype(F32)
        steer_rows = dot(one_hot_b, steer_p[c])
        out = tok_p[c].astype(F32) + total + gate * steer_rows
        lay_ref[:, j * 2 * rows : (j + 1) * 2 * rows] = out[:, : 2 * rows].astype(BF16)

    s_finish(1)
    s_copy(2).start()
    hg_copy.wait_recv()
    kv_back = (grad_kv[T:] + hgrecv[...].astype(F32)).astype(BF16)
    grad_all = jnp.concatenate(grad_query + [kv_back], axis=1)

    def g_copy(pair):
        return remote(
            gbuf.at[pair],
            grecv.at[h, pair % share],
            gsend.at[pair],
            grsem.at[h, pair % share],
            me,
            pair // share,
        )

    def g_step(i, total):
        c = ((h + 1) * share + i) % (S // 2)
        term = joined(dot_t(grad_all, qbuf[2 * c]), dot_t(grad_all, qbuf[2 * c + 1]))
        gbuf[c] = term

        @pl.when(c // share != h)
        def _():
            g_copy(c).start()

        return total + term.astype(F32) * vec_p[c, 0:1] * tok_p[c].astype(F32)

    row_terms = lax.fori_loop(0, S // 2, g_step, jnp.zeros(go_p.shape[1:], F32))
    row_own = jnp.sum(row_terms, axis=1, keepdims=True) * inverse
    as_row = jnp.sum(jnp.where(same, jnp.broadcast_to(row_own, (T, T)), 0.0), axis=0, keepdims=True)
    rbuf[...] = jnp.broadcast_to(as_row, rbuf.shape)

    def r_copy(d):
        return remote(rbuf, rrecv.at[h], rsend.at[d], rrsem.at[h], me, peers[d])

    for d in range(H - 1):
        r_copy(d).start()
    for k in range(2, steps):
        s_finish(k)
        if k + 1 < steps:
            s_copy(k + 1).start()

    def gate_step(c, total):
        return total + vec_p[c, 1:2] * vec_p[c, 0:1] * tok_p[c].astype(F32)

    gate_terms = lax.fori_loop(0, S // 2, gate_step, jnp.zeros(go_p.shape[1:], F32))
    row_total = row_own + grad_logit * inverse * jnp.sum(gate_terms, axis=1, keepdims=True)
    for j in range(share):
        sgrad_ref[:, j * 2 * rows : (j + 1) * 2 * rows] = sacc[steps, j][:, : 2 * rows]
    for peer in peers:
        remote(rbuf, rrecv.at[peer], rsend.at[0], rrsem.at[peer], me, peer).wait_recv()
        row_total = row_total + column(rrecv[peer, 0:1, :])
    row_mean = row_total * (1.0 / D)

    for j in range(share):
        c = h * share + j
        total = gbuf[c].astype(F32)
        for peer in peers:
            remote(
                gbuf.at[c], grecv.at[peer, j], gsend.at[c], grsem.at[peer, j], me, peer
            ).wait_recv()
            total = total + grecv[peer, j].astype(F32)
        scaled = (total + grad_logit * vec_p[c, 1:2]) * vec_p[c, 0:1]
        unit = tok_p[c].astype(F32) * inverse
        out = go_p[c].astype(F32) + inverse * (scaled - unit * row_mean)
        gtok_ref[:, j * 2 * rows : (j + 1) * 2 * rows] = out[:, : 2 * rows].astype(BF16)

    seg_copy.wait_send()
    kv_copy.wait_send()
    hg_copy.wait_send()
    for k in range(steps):
        s_copy(k).wait_send()
    for d in range(H - 1):
        r_copy(d).wait_send()

    def sent(i, carry):
        c = ((h + 1) * share + i) % (S // 2)
        a_copy(c).wait_send()
        g_copy(c).wait_send()
        return carry

    lax.fori_loop(0, S // 2 - share, sent, 0)
    for i in every:
        for way in range(3):
            q_copy(me, way, i).wait_send()
            o_copy(me, way, i).wait_send()

    def ring_sent(t, carry):
        a, b = at(pos + C - t), at(pos + t)
        for i in every:
            q_copy(a, 0, i).wait_send()
            o_copy(b, 1, i).wait_send()

            @pl.when(t < half - 1)
            def _():
                q_copy(b, 1, i).wait_send()
                o_copy(a, 0, i).wait_send()

            for slot in (a, b):
                q_copy(slot, 2, i).wait_send()
                o_copy(slot, 2, i).wait_send()
        return carry

    lax.fori_loop(1, half, ring_sent, 0)
    for i in every:
        q_copy(far, 2, i).wait_send()
        o_copy(far, 2, i).wait_send()


def shards(
    S,
    H,
    tokens,
    gain,
    w_query,
    w_key,
    w_value,
    w_out,
    w_gate,
    steering,
    segment_ids,
    steer_index,
    grad_out,
):
    T, D = tokens.shape
    rows, group_cols = w_query.shape
    hd = w_key.shape[1]
    heads = group_cols // hd
    wide = group_cols + 2 * hd
    pad = -(-rows // (16 * PIECES)) * 16 * PIECES
    pairs = S // H // 2
    pair_wide = -(-2 * rows // 128) * 128
    steps = S.bit_length() - 1
    steer_count = steering.shape[0]
    dma = pltpu.SemaphoreType.DMA
    vmem = pltpu.VMEM
    scratch = [
        vmem((S, pad, wide), BF16),
        vmem((S, pad, group_cols), BF16),
        vmem((S // 2, T, pair_wide), BF16),
        vmem((S // 2, T, pair_wide), BF16),
        vmem((S, T, pad), BF16),
        vmem((S, T, pad), BF16),
        vmem((S // 2, 2, pair_wide), F32),
        vmem((S // 2, steer_count, pair_wide), BF16),
        vmem((T, wide), F32),
        vmem((T, group_cols), F32),
        vmem((2 * T, 2 * hd), BF16),
        vmem((2, 8, T), jnp.int32),
        vmem((heads, T, 2 * T), F32),
        vmem((S // 2, T, pair_wide), BF16),
        vmem((H, pairs, T, pair_wide), BF16),
        vmem((S // 2, T, pair_wide), BF16),
        vmem((H, pairs, T, pair_wide), BF16),
        vmem((8, T), F32),
        vmem((H, 8, T), F32),
        vmem((T, 2 * hd), BF16),
        vmem((T, 2 * hd), BF16),
        vmem((steps + 1, pairs, steer_count, pair_wide), F32),
        vmem((steps, pairs, steer_count, pair_wide), F32),
        dma((3, S, PIECES)),
        dma((S, PIECES)),
        dma((3, S, PIECES)),
        dma((S, PIECES)),
        dma((2,)),
        dma((2,)),
        dma((2,)),
        dma((S // 2,)),
        dma((H, pairs)),
        dma((S // 2,)),
        dma((H, pairs)),
        dma((max(H - 1, 1),)),
        dma((H,)),
        dma((steps,)),
        dma((steps,)),
    ]
    return pl.pallas_call(
        functools.partial(kernel, S, H),
        out_shape=(
            jax.ShapeDtypeStruct((T, D // H), BF16),
            jax.ShapeDtypeStruct((T, D // H), BF16),
            jax.ShapeDtypeStruct((steer_count, D // H), F32),
        ),
        in_specs=[pl.BlockSpec(memory_space=pltpu.VMEM)] * 10,
        out_specs=[pl.BlockSpec(memory_space=pltpu.VMEM)] * 3,
        scratch_shapes=scratch,
        compiler_params=pltpu.CompilerParams(
            collective_id=0, has_side_effects=True, vmem_limit_bytes=50 * 1024 * 1024
        ),
    )(
        tokens,
        jnp.stack([gain, w_gate]),
        w_query,
        w_key,
        w_value,
        w_out,
        steering,
        segment_ids.reshape(1, T),
        steer_index.reshape(1, T),
        grad_out,
    )


def solution(mesh):
    placed = (
        P("seq", None),
        P(),
        P("seq", "head"),
        P("seq", "head"),
        P("seq", "head"),
        P("seq", "head"),
        P(),
        P(),
        P("seq"),
        P("seq"),
        P("seq", None),
    )
    return jax.shard_map(
        functools.partial(shards, mesh.shape["seq"], mesh.shape["head"]),
        mesh=mesh,
        in_specs=placed,
        out_specs=(P("seq", "head"), P("seq", "head"), P(None, "head")),
        check_vma=False,
    )
```

profile of v0, /device:TPU:0, one launch (start us, length us, event | category | flops | bytes accessed | tf_op | source)
XLA Modules:
  0.0 80.6 jit_solution(11175702105802061878)
XLA Ops:
  0.6 0.0 copy-start.8
  0.6 0.7 stack.9
  1.4 0.0 copy-done.8
  1.4 0.0 copy-start.6
  1.4 0.7 copy-done.6
  2.1 0.0 copy-start.7
  2.1 0.1 copy.15.wk_ref
  2.2 0.6 copy-done.7
  2.9 0.1 copy.16.wv_ref
  3.0 0.0 copy-start.5
  3.0 1.5 %copy.14.tok_ref = bf16[128,2880]{1,0:T(8,128)(2,1)S(1)} copy(bf16[128,2880]{0,1:T(8,128)(2,1)} %param.11) | data formatting | bytes 1474560 | tf_op args[0]
  4.5 0.0 copy-done.5
  4.5 0.0 copy-start
  4.6 0.0 copy-start.1
  4.6 0.0 copy-start.2
  4.6 0.0 copy-start.3
  4.6 0.0 copy-start.4
  4.6 0.3 copy.17.go_ref
  5.0 0.5 copy-done
  5.5 0.1 copy-done.1
  5.6 0.1 copy-done.2
  5.6 0.0 copy-done.3
  5.6 0.0 copy-done.4
  5.6 72.5 %shard_map.130 = (bf16[128,1440]{1,0:T(8,128)(2,1)S(1)}, bf16[128,1440]{1,0:T(8,128)(2,1)S(1)}, f32[16,1440]{1,0:T(8,128)S(1)}) custom-call(bf16[128,2880]{1,0:T(8,128)(2,1)S(1)} %copy.14.tok_ref, f32[2,2880]{1,0:T(2,128)S(1)} %pad_maximum_fusion.vec_ref, bf16[180,512]{1,0:T(8,128)(2,1)S(1)} %copy-done, bf16[180,64]{1,0:T(8,128)(2,1)S(1)} %copy.15.wk_ref, ...), custom_call_target="tpu_custom_call" | custom-call | tf_op jit(solution)/shard_map/pallas_call | solution.py:595
  78.1 0.9 %copy.18 = bf16[128,1440]{0,1:T(8,128)(2,1)} copy(bf16[128,1440]{1,0:T(8,128)(2,1)S(1)} %get-tuple-element.3) | data formatting | bytes 737280 | tf_op jit(solution)/shard_map/pallas_call | solution.py:595
  79.0 0.9 %copy.19 = bf16[128,1440]{0,1:T(8,128)(2,1)} copy(bf16[128,1440]{1,0:T(8,128)(2,1)S(1)} %get-tuple-element.4) | data formatting | bytes 737280 | tf_op jit(solution)/shard_map/pallas_call | solution.py:595
  80.0 0.6 copy.21
  (2 shorter events, 0.0 us)
Async XLA Ops:
  0.6 0.7 copy-start.8
  1.4 0.8 copy-start.6
  2.1 0.8 copy-start.7
  3.0 1.5 %copy-start.5 = (bf16[128,2880]{0,1:T(8,128)(2,1)S(1)}, bf16[128,2880]{0,1:T(8,128)(2,1)}, u32[]{:S(2)}) copy-start(bf16[128,2880]{0,1:T(8,128)(2,1)} %param.21) | copy-start | bytes 2211844
  4.5 0.9 %copy-start = (bf16[180,512]{1,0:T(8,128)(2,1)S(1)}, bf16[180,512]{1,0:T(8,128)(2,1)}, u32[]{:S(2)}) copy-start(bf16[180,512]{1,0:T(8,128)(2,1)} %wq_ref.1) | copy-start | bytes 552964
  4.6 1.0 %copy-start.1 = (bf16[180,512]{1,0:T(8,128)(2,1)S(1)}, bf16[180,512]{1,0:T(8,128)(2,1)}, u32[]{:S(2)}) copy-start(bf16[180,512]{1,0:T(8,128)(2,1)} %wo_ref.1) | copy-start | bytes 552964
  4.6 1.1 %copy-start.2 = (bf16[16,2880]{1,0:T(8,128)(2,1)S(1)}, bf16[16,2880]{1,0:T(8,128)(2,1)}, u32[]{:S(2)}) copy-start(bf16[16,2880]{1,0:T(8,128)(2,1)} %steer_ref.1) | copy-start | bytes 276484
  4.6 1.1 %copy-start.3 = (s32[128]{0:T(128)S(1)}, s32[128]{0:T(128)}, u32[]{:S(2)}) copy-start(s32[128]{0:T(128)} %param.19) | copy-start | bytes 1540
  4.6 1.0 %copy-start.4 = (s32[128]{0:T(128)S(1)}, s32[128]{0:T(128)}, u32[]{:S(2)}) copy-start(s32[128]{0:T(128)} %param.20) | copy-start | bytes 1540
where the time goes:
time: 80.9 us; the launch traced here: 80.6 us
  Pallas kernels  72.5 us (90%)
  local copies, waits for them, and re-layouts  7.36 us (9%)
    pallas_call x1, Pallas kernels, shards(): pl.pallas_call(functools.partial(kernel, S, H), out_shape=(jax.ShapeDtype...  72.5 us
    unnamed x23, local copies, waits for them, and re-layouts  4.79 us
    pallas_call x2, local copies, waits for them, and re-layouts, shards(): pl.pallas_call(functools.partial(kernel, S, H), out_shape=(jax.ShapeDtype...  1.83 us

commit v1 on v0

--- a/solution.py
+++ b/solution.py
@@ -32,7 +32,8 @@
     S,
     H,
     tok_ref,
-    vec_ref,
+    gain_ref,
+    wg_ref,
     wq_ref,
     wk_ref,
     wv_ref,
@@ -46,6 +47,10 @@
     sgrad_ref,
     qbuf,
     obuf,
+    tok_t,
+    go_t,
+    kv_t,
+    vec_t,
     tok_p,
     go_p,
     go_c,
@@ -82,10 +87,11 @@
     rrsem,
     ssend,
     srsem,
+    loadsem,
 ):
-    T, D = tok_ref.shape
+    D, T = tok_ref.shape
     rows, group_cols = wq_ref.shape
-    hd = wk_ref.shape[1]
+    hd = wk_ref.shape[0]
     heads = group_cols // hd
     scale = hd ** (-0.5)
     share = S // H // 2
@@ -125,6 +131,11 @@
         pairs.append(me + (1 - 2 * bit) * (1 << k))
     peers = [(h + d) % H for d in range(1, H)]
 
+    tok_load = pltpu.make_async_copy(tok_ref, tok_t, loadsem.at[0])
+    go_load = pltpu.make_async_copy(go_ref, go_t, loadsem.at[1])
+    tok_load.start()
+    go_load.start()
+
     barrier = pltpu.get_barrier_semaphore()
     for target in [cw, ccw, sib, after, before] + pairs:
         pl.semaphore_signal(barrier, inc=1, device_id=(target, h), device_id_type=MESH)
@@ -134,7 +145,10 @@
     qbuf[me] = jnp.zeros(qbuf.shape[1:], BF16)
     obuf[me] = jnp.zeros(obuf.shape[1:], BF16)
     qbuf[me, :rows, :group_cols] = wq_ref[...]
-    qbuf[me, :rows, group_cols:] = jnp.concatenate([wk_ref[...], wv_ref[...]], axis=1)
+    kv_t[...] = jnp.zeros(kv_t.shape, F32)
+    kv_t[:hd, :rows] = wk_ref[...].astype(F32)
+    kv_t[hd:, :rows] = wv_ref[...].astype(F32)
+    qbuf[me, :rows, group_cols:] = kv_t[...].T[:rows].astype(BF16)
     obuf[me, :rows, :] = wo_ref[...]
     segbuf[1] = jnp.broadcast_to(seg_ref[...], segbuf.shape[1:])
 
@@ -210,12 +224,45 @@
 
             o_copy(a, 2, i).start()
 
-    tokens = tok_ref[...].astype(F32)
-    inverse = lax.rsqrt(jnp.sum(tokens * tokens, axis=1, keepdims=True) * (1.0 / D) + EPSILON)
-    normed = (tokens * inverse * vec_ref[0:1, :]).astype(BF16)
-    norm_c[...] = jnp.zeros(norm_c.shape, BF16)
-    for c in range(S):
-        norm_c[c, :, :rows] = normed[:, c * rows : (c + 1) * rows]
+    same = lax.broadcasted_iota(jnp.int32, (T, T), 0) == lax.broadcasted_iota(jnp.int32, (T, T), 1)
+
+    def column(row):
+        return jnp.sum(
+            jnp.where(same, jnp.broadcast_to(row, (T, T)), 0), axis=1, keepdims=True
+        )
+
+    vec_t[0:1] = gain_ref[...].reshape(1, D)
+    vec_t[1:2] = wg_ref[...].reshape(1, D)
+    vec_p[...] = jnp.zeros(vec_p.shape, F32)
+    steer_p[...] = jnp.zeros(steer_p.shape, BF16)
+    for c in range(S // 2):
+        cols = slice(c * 2 * rows, (c + 1) * 2 * rows)
+        vec_p[c, :, : 2 * rows] = vec_t[:, cols]
+        steer_p[c, :, : 2 * rows] = steer_ref[:, cols]
+    gap = jnp.zeros((T, norm_c.shape[2] - rows), F32)
+
+    def halves(value):
+        low = jnp.concatenate([value[:, :rows], gap], axis=1)
+        high = jnp.concatenate([value[:, rows : 2 * rows], gap], axis=1)
+        return low.astype(BF16), high.astype(BF16)
+
+    def pair_rows(value, c):
+        fill = jnp.zeros((tok_p.shape[2] - 2 * rows, T), F32)
+        return jnp.concatenate([value[c * 2 * rows : (c + 1) * 2 * rows], fill], axis=0).T
+
+    tok_load.wait()
+    tokens = tok_t[...].astype(F32)
+    inverse = column(
+        lax.rsqrt(jnp.sum(tokens * tokens, axis=0, keepdims=True) * (1.0 / D) + EPSILON)
+    )
+    gate_sum = jnp.zeros(tok_p.shape[1:], F32)
+    for c in range(S // 2):
+        part = pair_rows(tokens, c)
+        tok_p[c] = part.astype(BF16)
+        normed = (part * inverse * vec_p[c, 0:1]).astype(BF16).astype(F32)
+        norm_c[2 * c], norm_c[2 * c + 1] = halves(normed)
+        gate_sum = gate_sum + normed * vec_p[c, 1:2]
+    gate = jax.nn.sigmoid(jnp.sum(gate_sum, axis=1, keepdims=True))
 
     def q_acc(slot):
         qacc[...] += dot(norm_c[slot], qbuf[slot])
@@ -235,19 +282,12 @@
     q_fwd(1)
     qacc[...] = dot(norm_c[me], qbuf[me])
     q_sib(sib)
-    gate = jax.nn.sigmoid(
-        jnp.sum(normed.astype(F32) * vec_ref[1:2, :], axis=1, keepdims=True)
-    )
-    for ref in (tok_p, go_p, go_c, vec_p, steer_p):
-        ref[...] = jnp.zeros(ref.shape, ref.dtype)
+    go_load.wait()
+    grads = go_t[...].astype(F32)
     for c in range(S // 2):
-        cols = slice(c * 2 * rows, (c + 1) * 2 * rows)
-        tok_p[c, :, : 2 * rows] = tok_ref[:, cols]
-        go_p[c, :, : 2 * rows] = go_ref[:, cols]
-        vec_p[c, :, : 2 * rows] = vec_ref[:, cols]
-        steer_p[c, :, : 2 * rows] = steer_ref[:, cols]
-    for c in range(S):
-        go_c[c, :, :rows] = go_ref[:, c * rows : (c + 1) * rows]
+        part = pair_rows(grads, c)
+        go_p[c] = part.astype(BF16)
+        go_c[2 * c], go_c[2 * c + 1] = halves(part)
 
     def q_both(t, carry):
         q_fwd(t)
@@ -273,11 +313,6 @@
     )
     kv_copy.start()
 
-    same = lax.broadcasted_iota(jnp.int32, (T, T), 0) == lax.broadcasted_iota(jnp.int32, (T, T), 1)
-
-    def column(row):
-        return jnp.sum(jnp.where(same, jnp.broadcast_to(row, (T, T)), 0), axis=1, keepdims=True)
-
     sidx_row = sidx_ref[...]
     sidx_col = column(sidx_row)
     one_hot_b = (
@@ -306,6 +341,14 @@
     def s_finish(k):
         s_copy(k).wait_recv()
         sacc[k + 1] = sacc[k] + srecv[k]
+
+    s_copy(0).start()
+
+    def gate_step(c, total):
+        return total + vec_p[c, 1:2] * vec_p[c, 0:1] * tok_p[c].astype(F32)
+
+    gate_terms = lax.fori_loop(0, S // 2, gate_step, jnp.zeros(go_p.shape[1:], F32))
+    row_gate = grad_logit * inverse * jnp.sum(gate_terms, axis=1, keepdims=True)
 
     seg_copy.wait_recv()
     halo_seg = jnp.where(me > 0, segbuf[0, 0:1, :], -1)
@@ -380,7 +423,8 @@
     for i in every:
         o_copy(far, 1, i).wait_recv()
         o_copy(far, 2, i).start()
-    s_copy(0).start()
+    s_finish(0)
+    s_copy(1).start()
     o_work(half - 1)
     o_acc(far)
 
@@ -401,8 +445,8 @@
     hgsend[...] = grad_kv[:T].astype(BF16)
     hg_copy = remote(hgsend, hgrecv, hgsem.at[0], hgsem.at[1], before, h)
     hg_copy.start()
-    s_finish(0)
-    s_copy(1).start()
+    s_finish(1)
+    s_copy(2).start()
 
     for j in range(share):
         c = h * share + j
@@ -416,8 +460,8 @@
         out = tok_p[c].astype(F32) + total + gate * steer_rows
         lay_ref[:, j * 2 * rows : (j + 1) * 2 * rows] = out[:, : 2 * rows].astype(BF16)
 
-    s_finish(1)
-    s_copy(2).start()
+    s_finish(2)
+    s_copy(3).start()
     hg_copy.wait_recv()
     kv_back = (grad_kv[T:] + hgrecv[...].astype(F32)).astype(BF16)
     grad_all = jnp.concatenate(grad_query + [kv_back], axis=1)
@@ -453,16 +497,12 @@
 
     for d in range(H - 1):
         r_copy(d).start()
-    for k in range(2, steps):
+    for k in range(3, steps):
         s_finish(k)
         if k + 1 < steps:
             s_copy(k + 1).start()
 
-    def gate_step(c, total):
-        return total + vec_p[c, 1:2] * vec_p[c, 0:1] * tok_p[c].astype(F32)
-
-    gate_terms = lax.fori_loop(0, S // 2, gate_step, jnp.zeros(go_p.shape[1:], F32))
-    row_total = row_own + grad_logit * inverse * jnp.sum(gate_terms, axis=1, keepdims=True)
+    row_total = row_own + row_gate
     for j in range(share):
         sgrad_ref[:, j * 2 * rows : (j + 1) * 2 * rows] = sacc[steps, j][:, : 2 * rows]
     for peer in peers:
@@ -555,6 +595,10 @@
     scratch = [
         vmem((S, pad, wide), BF16),
         vmem((S, pad, group_cols), BF16),
+        vmem((D, T), BF16),
+        vmem((D, T), BF16),
+        vmem((2 * hd, -(-rows // 128) * 128), F32),
+        vmem((2, D), F32),
         vmem((S // 2, T, pair_wide), BF16),
         vmem((S // 2, T, pair_wide), BF16),
         vmem((S, T, pad), BF16),
@@ -591,7 +635,10 @@
         dma((H,)),
         dma((steps,)),
         dma((steps,)),
+        dma((2,)),
     ]
+    on_chip = pl.BlockSpec(memory_space=pltpu.VMEM)
+    far_off = pl.BlockSpec(memory_space=pl.ANY)
     return pl.pallas_call(
         functools.partial(kernel, S, H),
         out_shape=(
@@ -599,23 +646,24 @@
             jax.ShapeDtypeStruct((T, D // H), BF16),
             jax.ShapeDtypeStruct((steer_count, D // H), F32),
         ),
-        in_specs=[pl.BlockSpec(memory_space=pltpu.VMEM)] * 10,
+        in_specs=[far_off] + [on_chip] * 9 + [far_off],
         out_specs=[pl.BlockSpec(memory_space=pltpu.VMEM)] * 3,
         scratch_shapes=scratch,
         compiler_params=pltpu.CompilerParams(
             collective_id=0, has_side_effects=True, vmem_limit_bytes=50 * 1024 * 1024
         ),
     )(
-        tokens,
-        jnp.stack([gain, w_gate]),
+        tokens.T,
+        gain,
+        w_gate,
         w_query,
-        w_key,
-        w_value,
+        w_key.T,
+        w_value.T,
         w_out,
         steering,
         segment_ids.reshape(1, T),
         steer_index.reshape(1, T),
-        grad_out,
+        grad_out.T,
     )
 
 

time: 80.9 us -> 85.4 us (1.056)
  local copies, waits for them, and re-layouts: 7.36 us -> 11 us
    unnamed x23, local copies, waits for them, and re-layouts: 4.79 us -> 9.19 us
where the time goes in v1:
time: 85.4 us; the launch traced here: 84.9 us
  Pallas kernels  73.2 us (86%)
  local copies, waits for them, and re-layouts  11 us (13%)
    pallas_call x1, Pallas kernels, shards(): pl.pallas_call(functools.partial(kernel, S, H), out_shape=(jax.ShapeDtype...  73.2 us
    unnamed x23, local copies, waits for them, and re-layouts  9.19 us
    pallas_call x2, local copies, waits for them, and re-layouts, shards(): pl.pallas_call(functools.partial(kernel, S, H), out_shape=(jax.ShapeDtype...  1.83 us

profile of v1, /device:TPU:0, one launch (start us, length us, event | category | flops | bytes accessed | tf_op | source)
XLA Modules:
  0.0 84.9 jit_solution(11877053223598434040)
XLA Ops:
  0.6 0.0 copy-start.9
  0.6 0.0 copy-start.10
  0.7 0.6 copy-done.9
  1.3 0.0 copy-done.10
  1.3 0.0 copy-start
  1.3 1.1 %copy-done = bf16[128,2880]{0,1:T(8,128)(2,1)S(1)} copy-done((bf16[128,2880]{0,1:T(8,128)(2,1)S(1)}, bf16[128,2880]{0,1:T(8,128)(2,1)}, u32[]{:S(2)}) %copy-start) | copy-done | bytes 737304
  2.4 0.0 copy-start.1
  2.4 1.1 %copy-done.1 = bf16[128,2880]{0,1:T(8,128)(2,1)S(1)} copy-done((bf16[128,2880]{0,1:T(8,128)(2,1)S(1)}, bf16[128,2880]{0,1:T(8,128)(2,1)}, u32[]{:S(2)}) %copy-start.1) | copy-done | bytes 737304
  3.5 0.0 copy-start.2
  3.5 0.9 %copy-done.2 = bf16[180,512]{1,0:T(8,128)(2,1)S(1)} copy-done((bf16[180,512]{1,0:T(8,128)(2,1)S(1)}, bf16[180,512]{1,0:T(8,128)(2,1)}, u32[]{:S(2)}) %copy-start.2) | copy-done | bytes 184344
  4.5 0.0 copy-start.3
  4.5 0.9 %copy-done.3 = bf16[180,512]{1,0:T(8,128)(2,1)S(1)} copy-done((bf16[180,512]{1,0:T(8,128)(2,1)S(1)}, bf16[180,512]{1,0:T(8,128)(2,1)}, u32[]{:S(2)}) %copy-start.3) | copy-done | bytes 184344
  5.4 0.0 copy-start.4
  5.4 0.9 %copy-done.4 = bf16[16,2880]{1,0:T(8,128)(2,1)S(1)} copy-done((bf16[16,2880]{1,0:T(8,128)(2,1)S(1)}, bf16[16,2880]{1,0:T(8,128)(2,1)}, u32[]{:S(2)}) %copy-start.4) | copy-done | bytes 92184
  6.3 0.0 copy-start.5
  6.3 0.8 copy-done.5
  7.0 0.0 copy-start.6
  7.0 0.8 copy-done.6
  7.8 0.0 copy-start.7
  7.8 0.7 copy-done.7
  8.5 0.0 copy-start.8
  8.5 0.7 copy-done.8
  9.2 73.2 %shard_map.130 = (bf16[128,1440]{1,0:T(8,128)(2,1)S(1)}, bf16[128,1440]{1,0:T(8,128)(2,1)S(1)}, f32[16,1440]{1,0:T(8,128)S(1)}) custom-call(bf16[2880,128]{1,0:T(8,128)(2,1)S(1)} %bitcast.6, f32[2880]{0:T(1024)S(1)} %copy-done.7, f32[2880]{0:T(1024)S(1)} %copy-done.8, bf16[180,512]{1,0:T(8,128)(2,1)S(1)} %copy-done.2, bf16[64,180]{1,0:T(8,128)(2,1)S(1)} %bitcast.8, ...), custom_call_target="tpu_custom_call" | custom-call | tf_op jit(solution)/shard_map/pallas_call | solution.py:642
  82.4 0.9 %copy.14 = bf16[128,1440]{0,1:T(8,128)(2,1)} copy(bf16[128,1440]{1,0:T(8,128)(2,1)S(1)} %get-tuple-element.3) | data formatting | bytes 737280 | tf_op jit(solution)/shard_map/pallas_call | solution.py:642
  83.3 0.9 %copy.15 = bf16[128,1440]{0,1:T(8,128)(2,1)} copy(bf16[128,1440]{1,0:T(8,128)(2,1)S(1)} %get-tuple-element.4) | data formatting | bytes 737280 | tf_op jit(solution)/shard_map/pallas_call | solution.py:642
  84.2 0.6 copy.17
Async XLA Ops:
  0.6 0.7 copy-start.9
  0.6 0.7 copy-start.10
  1.3 1.1 %copy-start = (bf16[128,2880]{0,1:T(8,128)(2,1)S(1)}, bf16[128,2880]{0,1:T(8,128)(2,1)}, u32[]{:S(2)}) copy-start(bf16[128,2880]{0,1:T(8,128)(2,1)} %param.11) | copy-start | bytes 2211844
  2.4 1.1 %copy-start.1 = (bf16[128,2880]{0,1:T(8,128)(2,1)S(1)}, bf16[128,2880]{0,1:T(8,128)(2,1)}, u32[]{:S(2)}) copy-start(bf16[128,2880]{0,1:T(8,128)(2,1)} %param.21) | copy-start | bytes 2211844
  3.5 0.9 %copy-start.2 = (bf16[180,512]{1,0:T(8,128)(2,1)S(1)}, bf16[180,512]{1,0:T(8,128)(2,1)}, u32[]{:S(2)}) copy-start(bf16[180,512]{1,0:T(8,128)(2,1)} %wq_ref.1) | copy-start | bytes 552964
  4.5 0.9 %copy-start.3 = (bf16[180,512]{1,0:T(8,128)(2,1)S(1)}, bf16[180,512]{1,0:T(8,128)(2,1)}, u32[]{:S(2)}) copy-start(bf16[180,512]{1,0:T(8,128)(2,1)} %wo_ref.1) | copy-start | bytes 552964
  5.4 0.9 %copy-start.4 = (bf16[16,2880]{1,0:T(8,128)(2,1)S(1)}, bf16[16,2880]{1,0:T(8,128)(2,1)}, u32[]{:S(2)}) copy-start(bf16[16,2880]{1,0:T(8,128)(2,1)} %steer_ref.1) | copy-start | bytes 276484
  6.3 0.8 copy-start.5
  7.0 0.8 copy-start.6
  7.8 0.7 copy-start.7
  8.5 0.7 copy-start.8

commit v2 on v1

--- a/solution.py
+++ b/solution.py
@@ -31,7 +31,23 @@
 def kernel(
     S,
     H,
-    tok_ref,
+    tok_any,
+    gain_any,
+    wg_any,
+    wq_any,
+    wk_any,
+    wv_any,
+    wo_any,
+    steer_any,
+    seg_any,
+    sidx_any,
+    go_any,
+    lay_ref,
+    gtok_ref,
+    sgrad_ref,
+    qbuf,
+    obuf,
+    tok_t,
     gain_ref,
     wg_ref,
     wq_ref,
@@ -41,13 +57,6 @@
     steer_ref,
     seg_ref,
     sidx_ref,
-    go_ref,
-    lay_ref,
-    gtok_ref,
-    sgrad_ref,
-    qbuf,
-    obuf,
-    tok_t,
     go_t,
     kv_t,
     vec_t,
@@ -89,7 +98,7 @@
     srsem,
     loadsem,
 ):
-    D, T = tok_ref.shape
+    D, T = tok_any.shape
     rows, group_cols = wq_ref.shape
     hd = wk_ref.shape[0]
     heads = group_cols // hd
@@ -131,10 +140,24 @@
         pairs.append(me + (1 - 2 * bit) * (1 << k))
     peers = [(h + d) % H for d in range(1, H)]
 
-    tok_load = pltpu.make_async_copy(tok_ref, tok_t, loadsem.at[0])
-    go_load = pltpu.make_async_copy(go_ref, go_t, loadsem.at[1])
-    tok_load.start()
-    go_load.start()
+    loads = {}
+    for i, (name, src, dst) in enumerate(
+        [
+            ("wq", wq_any, wq_ref),
+            ("wk", wk_any, wk_ref),
+            ("wv", wv_any, wv_ref),
+            ("wo", wo_any, wo_ref),
+            ("seg", seg_any, seg_ref),
+            ("tok", tok_any, tok_t),
+            ("gain", gain_any, gain_ref),
+            ("wg", wg_any, wg_ref),
+            ("steer", steer_any, steer_ref),
+            ("sidx", sidx_any, sidx_ref),
+            ("go", go_any, go_t),
+        ]
+    ):
+        loads[name] = pltpu.make_async_copy(src, dst, loadsem.at[i])
+        loads[name].start()
 
     barrier = pltpu.get_barrier_semaphore()
     for target in [cw, ccw, sib, after, before] + pairs:
@@ -144,8 +167,10 @@
 
     qbuf[me] = jnp.zeros(qbuf.shape[1:], BF16)
     obuf[me] = jnp.zeros(obuf.shape[1:], BF16)
+    kv_t[...] = jnp.zeros(kv_t.shape, F32)
+    for name in ("wq", "wk", "wv", "wo", "seg"):
+        loads[name].wait()
     qbuf[me, :rows, :group_cols] = wq_ref[...]
-    kv_t[...] = jnp.zeros(kv_t.shape, F32)
     kv_t[:hd, :rows] = wk_ref[...].astype(F32)
     kv_t[hd:, :rows] = wv_ref[...].astype(F32)
     qbuf[me, :rows, group_cols:] = kv_t[...].T[:rows].astype(BF16)
@@ -231,6 +256,8 @@
             jnp.where(same, jnp.broadcast_to(row, (T, T)), 0), axis=1, keepdims=True
         )
 
+    for name in ("gain", "wg", "steer", "sidx"):
+        loads[name].wait()
     vec_t[0:1] = gain_ref[...].reshape(1, D)
     vec_t[1:2] = wg_ref[...].reshape(1, D)
     vec_p[...] = jnp.zeros(vec_p.shape, F32)
@@ -250,7 +277,7 @@
         fill = jnp.zeros((tok_p.shape[2] - 2 * rows, T), F32)
         return jnp.concatenate([value[c * 2 * rows : (c + 1) * 2 * rows], fill], axis=0).T
 
-    tok_load.wait()
+    loads["tok"].wait()
     tokens = tok_t[...].astype(F32)
     inverse = column(
         lax.rsqrt(jnp.sum(tokens * tokens, axis=0, keepdims=True) * (1.0 / D) + EPSILON)
@@ -282,7 +309,7 @@
     q_fwd(1)
     qacc[...] = dot(norm_c[me], qbuf[me])
     q_sib(sib)
-    go_load.wait()
+    loads["go"].wait()
     grads = go_t[...].astype(F32)
     for c in range(S // 2):
         part = pair_rows(grads, c)
@@ -596,6 +623,15 @@
         vmem((S, pad, wide), BF16),
         vmem((S, pad, group_cols), BF16),
         vmem((D, T), BF16),
+        vmem((D,), F32),
+        vmem((D,), F32),
+        vmem((rows, group_cols), BF16),
+        vmem((hd, rows), BF16),
+        vmem((hd, rows), BF16),
+        vmem((rows, group_cols), BF16),
+        vmem((steer_count, D), BF16),
+        vmem((1, T), jnp.int32),
+        vmem((1, T), jnp.int32),
         vmem((D, T), BF16),
         vmem((2 * hd, -(-rows // 128) * 128), F32),
         vmem((2, D), F32),
@@ -635,9 +671,8 @@
         dma((H,)),
         dma((steps,)),
         dma((steps,)),
-        dma((2,)),
+        dma((11,)),
     ]
-    on_chip = pl.BlockSpec(memory_space=pltpu.VMEM)
     far_off = pl.BlockSpec(memory_space=pl.ANY)
     return pl.pallas_call(
         functools.partial(kernel, S, H),
@@ -646,11 +681,11 @@
             jax.ShapeDtypeStruct((T, D // H), BF16),
             jax.ShapeDtypeStruct((steer_count, D // H), F32),
         ),
-        in_specs=[far_off] + [on_chip] * 9 + [far_off],
+        in_specs=[far_off] * 11,
         out_specs=[pl.BlockSpec(memory_space=pltpu.VMEM)] * 3,
         scratch_shapes=scratch,
         compiler_params=pltpu.CompilerParams(
-            collective_id=0, has_side_effects=True, vmem_limit_bytes=50 * 1024 * 1024
+            collective_id=0, has_side_effects=True, vmem_limit_bytes=60 * 1024 * 1024
         ),
     )(
         tokens.T,

time: 85.4 us -> 78 us (0.913)
  local copies, waits for them, and re-layouts: 11 us -> 3.53 us
    unnamed x23 -> x5, local copies, waits for them, and re-layouts: 9.19 us -> 0.65 us
    pallas_call x2, local copies, waits for them, and re-layouts: 1.83 us -> 2.88 us  [shards(): pl.pallas_call(functools.partial(kernel, S, H), out_shape=(jax.ShapeDtype...]
where the time goes in v2:
time: 78 us; the launch traced here: 77.8 us
  Pallas kernels  73.7 us (94%)
  local copies, waits for them, and re-layouts  3.53 us (5%)
    pallas_call x1, Pallas kernels, shards(): pl.pallas_call(functools.partial(kernel, S, H), out_shape=(jax.ShapeDtype...  73.7 us
    pallas_call x2, local copies, waits for them, and re-layouts, shards(): pl.pallas_call(functools.partial(kernel, S, H), out_shape=(jax.ShapeDtype...  2.88 us

profile of v2, /device:TPU:0, one launch (start us, length us, event | category | flops | bytes accessed | tf_op | source)
XLA Modules:
  0.0 77.8 jit_solution(10881282014311182666)
XLA Ops:
  0.6 73.7 %shard_map.130 = (bf16[128,1440]{1,0:T(8,128)(2,1)}, bf16[128,1440]{1,0:T(8,128)(2,1)}, f32[16,1440]{1,0:T(8,128)}) custom-call(bf16[2880,128]{1,0:T(8,128)(2,1)} %bitcast.6, f32[2880]{0:T(1024)} %gain_any.1, f32[2880]{0:T(1024)} %wg_any.1, bf16[180,512]{1,0:T(8,128)(2,1)} %wq_any.1, bf16[64,180]{1,0:T(8,128)(2,1)} %bitcast.8, bf16[64,180]{1,0:T(8,128)(2,1)} %bitcast.9, ...), custom_call_target="tpu_custom_call" | custom-call | tf_op jit(solution)/shard_map/pallas_call | solution.py:677
  74.3 0.0 copy-start
  74.3 2.0 %copy.14 = bf16[128,1440]{0,1:T(8,128)(2,1)} copy(bf16[128,1440]{1,0:T(8,128)(2,1)} %get-tuple-element.3) | data formatting | bytes 737280 | tf_op jit(solution)/shard_map/pallas_call | solution.py:677
  76.3 0.0 copy-done
  76.3 0.0 copy-start.1
  76.3 0.9 %copy.15 = bf16[128,1440]{0,1:T(8,128)(2,1)} copy(bf16[128,1440]{1,0:T(8,128)(2,1)S(1)} %copy-done) | data formatting | bytes 737280 | tf_op jit(solution)/shard_map/pallas_call | solution.py:677
  77.2 0.0 copy-done.1
  77.2 0.6 copy.17
Async XLA Ops:
  74.3 2.0 %copy-start = (bf16[128,1440]{1,0:T(8,128)(2,1)S(1)}, bf16[128,1440]{1,0:T(8,128)(2,1)}, u32[]{:S(2)}) copy-start(bf16[128,1440]{1,0:T(8,128)(2,1)} %get-tuple-element.4) | copy-start | bytes 1105924
  76.3 0.9 %copy-start.1 = (f32[16,1440]{1,0:T(8,128)S(1)}, f32[16,1440]{1,0:T(8,128)}, u32[]{:S(2)}) copy-start(f32[16,1440]{1,0:T(8,128)} %get-tuple-element.11) | copy-start | bytes 276484

commit v3 on v2

--- a/solution.py
+++ b/solution.py
@@ -97,6 +97,7 @@
     ssend,
     srsem,
     loadsem,
+    out_t,
 ):
     D, T = tok_any.shape
     rows, group_cols = wq_ref.shape
@@ -404,11 +405,11 @@
             o_fwd(1)
         if i == heads - 1:
             o_fwd(2)
-    mixed = jnp.concatenate(mixed_parts, axis=1)
+    mixed_t = jnp.concatenate(mixed_parts, axis=1).astype(F32).T.astype(BF16)
 
     def joined(low, high):
-        fill = jnp.zeros((T, abuf.shape[2] - 2 * rows), F32)
-        return jnp.concatenate([low[:, :rows], high[:, :rows], fill], axis=1).astype(BF16)
+        fill = jnp.zeros((abuf.shape[2] - 2 * rows, T), F32)
+        return jnp.concatenate([low[:rows], high[:rows], fill], axis=0).T.astype(BF16)
 
     def a_copy(pair):
         return remote(
@@ -425,7 +426,7 @@
             o_copy(slot + other, 2, i).wait_recv()
         pair = slot // 2
         low, high = obuf[2 * pair], obuf[2 * pair + 1]
-        abuf[pair] = joined(dot_t(mixed, low), dot_t(mixed, high))
+        abuf[pair] = joined(dot(low, mixed_t), dot(high, mixed_t))
 
         @pl.when(pair // share != h)
         def _():
@@ -485,13 +486,14 @@
             total = total + arecv[peer, j].astype(F32)
         steer_rows = dot(one_hot_b, steer_p[c])
         out = tok_p[c].astype(F32) + total + gate * steer_rows
-        lay_ref[:, j * 2 * rows : (j + 1) * 2 * rows] = out[:, : 2 * rows].astype(BF16)
+        out_t[j * 2 * rows : (j + 1) * 2 * rows] = out.T[: 2 * rows]
+    lay_ref[...] = out_t[...].astype(BF16)
 
     s_finish(2)
     s_copy(3).start()
     hg_copy.wait_recv()
     kv_back = (grad_kv[T:] + hgrecv[...].astype(F32)).astype(BF16)
-    grad_all = jnp.concatenate(grad_query + [kv_back], axis=1)
+    grad_t = jnp.concatenate(grad_query + [kv_back], axis=1).astype(F32).T.astype(BF16)
 
     def g_copy(pair):
         return remote(
@@ -505,7 +507,7 @@
 
     def g_step(i, total):
         c = ((h + 1) * share + i) % (S // 2)
-        term = joined(dot_t(grad_all, qbuf[2 * c]), dot_t(grad_all, qbuf[2 * c + 1]))
+        term = joined(dot(qbuf[2 * c], grad_t), dot(qbuf[2 * c + 1], grad_t))
         gbuf[c] = term
 
         @pl.when(c // share != h)
@@ -548,7 +550,8 @@
         scaled = (total + grad_logit * vec_p[c, 1:2]) * vec_p[c, 0:1]
         unit = tok_p[c].astype(F32) * inverse
         out = go_p[c].astype(F32) + inverse * (scaled - unit * row_mean)
-        gtok_ref[:, j * 2 * rows : (j + 1) * 2 * rows] = out[:, : 2 * rows].astype(BF16)
+        out_t[j * 2 * rows : (j + 1) * 2 * rows] = out.T[: 2 * rows]
+    gtok_ref[...] = out_t[...].astype(BF16)
 
     seg_copy.wait_send()
     kv_copy.wait_send()
@@ -672,13 +675,14 @@
         dma((steps,)),
         dma((steps,)),
         dma((11,)),
+        vmem((D // H, T), F32),
     ]
     far_off = pl.BlockSpec(memory_space=pl.ANY)
-    return pl.pallas_call(
+    layer_t, grad_t, steer_grad = pl.pallas_call(
         functools.partial(kernel, S, H),
         out_shape=(
-            jax.ShapeDtypeStruct((T, D // H), BF16),
-            jax.ShapeDtypeStruct((T, D // H), BF16),
+            jax.ShapeDtypeStruct((D // H, T), BF16),
+            jax.ShapeDtypeStruct((D // H, T), BF16),
             jax.ShapeDtypeStruct((steer_count, D // H), F32),
         ),
         in_specs=[far_off] * 11,
@@ -700,6 +704,7 @@
         steer_index.reshape(1, T),
         grad_out.T,
     )
+    return layer_t.T, grad_t.T, steer_grad
 
 
 def solution(mesh):

time: 78 us -> 78 us (level)
    pallas_call x2 -> x0, local copies, waits for them, and re-layouts: 2.88 us -> none  [shards(): pl.pallas_call(functools.partial(kernel, S, H), out_shape=(jax.ShapeDtype...]
    unnamed x5 -> x7, local copies, waits for them, and re-layouts: 0.65 us -> 3.4 us
where the time goes in v3:
time: 78 us; the launch traced here: 77.8 us
  Pallas kernels  73.8 us (95%)
  local copies, waits for them, and re-layouts  3.4 us (4%)
    pallas_call x1, Pallas kernels, shards(): pl.pallas_call(functools.partial(kernel, S, H), out_shape=(jax.ShapeDtype...  73.8 us
    unnamed x7, local copies, waits for them, and re-layouts  3.4 us

profile of v3, /device:TPU:0, one launch (start us, length us, event | category | flops | bytes accessed | tf_op | source)
XLA Modules:
  0.0 77.8 jit_solution(2328804553129334053)
XLA Ops:
  0.6 73.8 %shard_map.130 = (bf16[1440,128]{1,0:T(8,128)(2,1)}, bf16[1440,128]{1,0:T(8,128)(2,1)}, f32[16,1440]{1,0:T(8,128)}) custom-call(bf16[2880,128]{1,0:T(8,128)(2,1)} %bitcast.8, f32[2880]{0:T(1024)} %gain_any.1, f32[2880]{0:T(1024)} %wg_any.1, bf16[180,512]{1,0:T(8,128)(2,1)} %wq_any.1, bf16[64,180]{1,0:T(8,128)(2,1)} %bitcast.12, bf16[64,180]{1,0:T(8,128)(2,1)} %bitcast.13, ...), custom_call_target="tpu_custom_call" | custom-call | tf_op jit(solution)/shard_map/pallas_call | solution.py:681
  74.4 0.0 copy-start
  74.4 1.8 %copy.17 = bf16[128,1440]{0,1:T(8,128)(2,1)} copy(bf16[128,1440]{0,1:T(8,128)(2,1)} %bitcast.11) | data formatting | bytes 737280
  76.2 0.0 copy-done
  76.2 0.0 copy-start.1
  76.2 0.7 copy.18
  77.0 0.2 copy-done.1
  77.2 0.6 copy.19
Async XLA Ops:
  74.4 1.8 %copy-start = (bf16[1440,128]{1,0:T(8,128)(2,1)S(1)}, bf16[1440,128]{1,0:T(8,128)(2,1)}, u32[]{:S(2)}) copy-start(bf16[1440,128]{1,0:T(8,128)(2,1)} %get-tuple-element.7) | copy-start | bytes 1105924
  76.2 1.0 %copy-start.1 = (f32[16,1440]{1,0:T(8,128)S(1)}, f32[16,1440]{1,0:T(8,128)}, u32[]{:S(2)}) copy-start(f32[16,1440]{1,0:T(8,128)} %get-tuple-element.14) | copy-start | bytes 276484

commit v4 on v3

--- a/solution.py
+++ b/solution.py
@@ -308,6 +308,9 @@
         q_sib(b + other)
 
     q_fwd(1)
+    for i in every:
+        for way in range(3):
+            o_copy(me, way, i).start()
     qacc[...] = dot(norm_c[me], qbuf[me])
     q_sib(sib)
     loads["go"].wait()
@@ -323,9 +326,6 @@
         return carry
 
     lax.fori_loop(2, half, q_both, 0)
-    for i in every:
-        for way in range(3):
-            o_copy(me, way, i).start()
     q_work(half - 1)
     far = at(pos + half)
     for i in every:

time: 78 us -> 81.1 us (1.040)
  Pallas kernels: 73.8 us -> 76.9 us
    pallas_call x1, Pallas kernels: 73.8 us -> 76.9 us  [shards(): pl.pallas_call(functools.partial(kernel, S, H), out_shape=(jax.ShapeDtype...]
where the time goes in v4:
time: 81.1 us; the launch traced here: 80.9 us
  Pallas kernels  76.9 us (95%)
  local copies, waits for them, and re-layouts  3.4 us (4%)
    pallas_call x1, Pallas kernels, shards(): pl.pallas_call(functools.partial(kernel, S, H), out_shape=(jax.ShapeDtype...  76.9 us
    unnamed x7, local copies, waits for them, and re-layouts  3.4 us

profile of v4, /device:TPU:0, one launch (start us, length us, event | category | flops | bytes accessed | tf_op | source)
XLA Modules:
  0.0 80.9 jit_solution(168697221305894373)
XLA Ops:
  0.6 76.9 %shard_map.130 = (bf16[1440,128]{1,0:T(8,128)(2,1)}, bf16[1440,128]{1,0:T(8,128)(2,1)}, f32[16,1440]{1,0:T(8,128)}) custom-call(bf16[2880,128]{1,0:T(8,128)(2,1)} %bitcast.8, f32[2880]{0:T(1024)} %gain_any.1, f32[2880]{0:T(1024)} %wg_any.1, bf16[180,512]{1,0:T(8,128)(2,1)} %wq_any.1, bf16[64,180]{1,0:T(8,128)(2,1)} %bitcast.12, bf16[64,180]{1,0:T(8,128)(2,1)} %bitcast.13, ...), custom_call_target="tpu_custom_call" | custom-call | tf_op jit(solution)/shard_map/pallas_call | solution.py:681
  77.5 0.0 copy-start
  77.5 1.8 %copy.17 = bf16[128,1440]{0,1:T(8,128)(2,1)} copy(bf16[128,1440]{0,1:T(8,128)(2,1)} %bitcast.11) | data formatting | bytes 737280
  79.3 0.0 copy-done
  79.3 0.0 copy-start.1
  79.3 0.7 copy.18
  80.1 0.2 copy-done.1
  80.3 0.6 copy.19
Async XLA Ops:
  77.5 1.8 %copy-start = (bf16[1440,128]{1,0:T(8,128)(2,1)S(1)}, bf16[1440,128]{1,0:T(8,128)(2,1)}, u32[]{:S(2)}) copy-start(bf16[1440,128]{1,0:T(8,128)(2,1)} %get-tuple-element.7) | copy-start | bytes 1105924
  79.3 1.0 %copy-start.1 = (f32[16,1440]{1,0:T(8,128)S(1)}, f32[16,1440]{1,0:T(8,128)}, u32[]{:S(2)}) copy-start(f32[16,1440]{1,0:T(8,128)} %get-tuple-element.14) | copy-start | bytes 276484
